TPU v7x, 32 devices: a whole 2x2x4 slice. The times are simulated.
32 devices in a mesh: group: 2 (over y), expert: 4 (over z), tensor: 2 (over x), pipe: 2 (over core).
Axes of the slice: x: 2, y: 2, z: 4, core: 2. Of those that a mesh axis runs over, the one named last changes fastest.
Arguments:
- attn_terms: bfloat16 [2, 320, 3584], P('tensor', ('group', 'expert')), parts along dimension 1, may hold values from -4 to 4
- residual: bfloat16 [320, 3584], P(('group', 'expert')), parts along dimension 0, may hold values from -10.5 to 10.5
- norm_gain: float32 [3584], replicated, may hold values from 0.5 to 1.5
- routes: int32 [320, 8], P(('group', 'expert')), parts along dimension 0, may hold values from 0 to 31, all different within a row; in each aligned block of 40 rows (0 to 39, 40 to 79, ...) at most 15 rows name the same one
- gate_scores: float32 [320, 8], P(('group', 'expert')), parts along dimension 0, may hold values from 0.05 to 1
- gate_weight: bfloat16 [32, 3584, 1024], P('expert', None, ('tensor', 'pipe')), may hold values from -0.09375 to 0.09375
- up_weight: bfloat16 [32, 3584, 1024], P('expert', None, ('tensor', 'pipe')), may hold values from -0.09375 to 0.09375
- down_weight: bfloat16 [32, 1024, 3584], P('expert', ('tensor', 'pipe')), may hold values from -0.1875 to 0.1875
Outputs:
- layer_out: bfloat16 [320, 3584], P(('group', 'expert'), ('tensor', 'pipe')), parts along dimension 0
There are 2 independent parts, one for each index of `group`. A program takes and returns all parts, laid end to end along the dimension named above; an argument that names none is the same for every part. Nothing has to cross between parts.
Inputs may be any that keep to these rules, and one draw needn't show every extreme that they name: `routes`: each row names 8 different experts. Within each aligned block of 40 rows (the rows of one index of expert) no expert is named more than 15 times, a bound that some block reaches.
All inputs are finite; a program needn't handle non-finite values.
Results may differ from a plain program's by a relative error of at most 0.013.
Values may be sent and summed in bfloat16 or wider, within the bound.
A program may use at most 128 MiB of HBM per device.

v0:
```python
import jax
import jax.numpy as jnp
from jax import lax
from jax.sharding import PartitionSpec as P

EXPERTS = 32
TOP = 8
CAP = 15


ROUTE_SCALE = 2.5
NORM_EPS = 1e-06


def slot_positions(routes):
    row_count, top_count = routes.shape
    flat_routes = routes.reshape(row_count * top_count)
    onehot = (flat_routes[:, None] == jnp.arange(EXPERTS, dtype=jnp.int32)[None, :]).astype(
        jnp.int32
    )
    before = jnp.cumsum(onehot, axis=0) - onehot
    slot_index = jnp.sum(before * onehot, axis=1)
    return (flat_routes * CAP + slot_index).reshape(row_count, top_count)


def shards(
    attn_terms, residual, norm_gain, routes, gate_scores, gate_weight, up_weight, down_weight
):
    tensor_count = lax.axis_size("tensor")
    pipe_count = lax.axis_size("pipe")
    group_count = tensor_count * pipe_count
    model_width = residual.shape[1]
    piece_width = model_width // group_count
    tensor_pos = lax.axis_index("tensor")
    pipe_pos = lax.axis_index("pipe")
    group_pos = tensor_pos * pipe_count + pipe_pos
    partial_terms = attn_terms[0].astype(jnp.float32)
    attn_sum = lax.psum(partial_terms.astype(jnp.bfloat16), "tensor").astype(jnp.float32)
    hidden_state = residual.astype(jnp.float32) + attn_sum
    inv_rms = lax.rsqrt(jnp.mean(hidden_state * hidden_state, axis=1, keepdims=True) + NORM_EPS)
    normed = (hidden_state * inv_rms * norm_gain[None, :]).astype(jnp.bfloat16)
    own_state = lax.dynamic_slice_in_dim(hidden_state, group_pos * piece_width, piece_width, 1)
    mix_weight = ROUTE_SCALE * gate_scores / jnp.sum(gate_scores, axis=1, keepdims=True)
    positions = slot_positions(routes)
    slot_total = EXPERTS * CAP
    slot_ids = jnp.arange(slot_total, dtype=jnp.int32)[None, :]
    placement_matrix = jnp.zeros((routes.shape[0], slot_total), jnp.bfloat16)
    for choice_index in range(TOP):
        placement_matrix = placement_matrix + (
            positions[:, choice_index : choice_index + 1] == slot_ids
        ).astype(jnp.bfloat16)
    send_buffer = lax.dot_general(
        placement_matrix, normed, (((0,), (0,)), ((), ())), preferred_element_type=jnp.float32
    )
    send_buffer = send_buffer.astype(jnp.bfloat16).reshape(EXPERTS, CAP, normed.shape[1])
    received = lax.all_to_all(send_buffer, "expert", split_axis=0, concat_axis=1, tiled=True)
    gate_sums = jnp.einsum(
        "erd,edf->erf", received, gate_weight, preferred_element_type=jnp.float32
    )
    up_sums = jnp.einsum("erd,edf->erf", received, up_weight, preferred_element_type=jnp.float32)
    expert_hidden = (jax.nn.silu(gate_sums) * up_sums).astype(jnp.bfloat16)
    partial_out = jnp.einsum(
        "erf,efd->erd", expert_hidden, down_weight, preferred_element_type=jnp.float32
    ).astype(jnp.bfloat16)
    returned = lax.all_to_all(partial_out, "expert", split_axis=1, concat_axis=0, tiled=True)
    flat_rows = returned.reshape(EXPERTS * CAP, returned.shape[2])
    picked = flat_rows[positions]
    weighted = jnp.einsum("rk,rkd->rd", mix_weight, picked.astype(jnp.float32))
    combined = lax.psum_scatter(
        weighted.astype(jnp.bfloat16), ("tensor", "pipe"), scatter_dimension=1, tiled=True
    ).astype(jnp.float32)
    return (own_state + combined).astype(jnp.bfloat16)


def solution(mesh):
    placed = (
        P("tensor", ("group", "expert"), None),
        P(("group", "expert"), None),
        P(),
        P(("group", "expert"), None),
        P(("group", "expert"), None),
        P("expert", None, ("tensor", "pipe")),
        P("expert", None, ("tensor", "pipe")),
        P("expert", ("tensor", "pipe"), None),
    )
    return jax.shard_map(
        shards,
        mesh=mesh,
        in_specs=placed,
        out_specs=P(("group", "expert"), ("tensor", "pipe")),
        check_vma=False,
    )
```

profile of v0, /device:TPU:0, one launch (start us, length us, event | category | flops | bytes accessed | tf_op | source)
XLA Modules:
  0.0 287.3 jit_solution(18181446347671061715)
XLA Ops:
  6.5 0.7 all-reduce.3.cloned.1.call-update
  7.3 0.8 copy.28
  8.0 0.1 eq.142
  8.1 0.9 reduce-window.6
  9.0 0.2 slice_reduce_fusion
  9.3 0.1 bitcast_bitcast_fusion
  9.4 0.1 reduce_sum.31
  9.5 0.3 slice_reduce_fusion.8
  9.8 26.1 %all-reduce.3.cloned.1.call-done = bf16[40,3584]{1,0:T(8,128)(2,1)} async-done(((bf16[40,3584]{1,0:T(8,128)(2,1)}), bf16[40,3584]{1,0:T(8,128)(2,1)}) %all-reduce.3.cloned.1.call-update) | async-done | bytes 286736 | tf_op jit(solution)/shard_map/psum | solution.py:38
  35.9 2.1 convert_add_fusion
  38.0 2.3 convolution_convert_fusion.1
  40.3 2.8 reshape.34
  43.0 86.3 %all_to_all.33 = bf16[32,15,3584]{2,1,0:T(8,128)(2,1)S(1)} all-to-all(bf16[32,15,3584]{2,1,0:T(8,128)(2,1)} %reshape.34), channel_id=1, replica_groups=mesh['group'=2,'expert'=4,'tensor'=2,'pipe'=2] {'expert'}, dimensions={0} | all-to-all | bytes 6881280 | tf_op jit(solution)/shard_map/all_to_all | solution.py:56
  129.3 2.0 copy.32
  131.3 8.4 %fusion.2 = f32[8,60,256]{2,1,0:T(8,128)} fusion(bf16[8,3584,256]{2,1,0:T(8,128)(2,1)} %param.13, bf16[8,60,3584]{2,0,1:T(8,128)(2,1)S(1)} %bitcast.40), kind=kOutput, calls=%fused_computation.5 | convolution fusion | flops 880803840 | bytes 18612224 | tf_op jit(solution)/shard_map/erd,edf->erf/dot_general | solution.py:57
  139.8 16.5 %convolution_convert_fusion = bf16[8,60,3584]{2,1,0:T(8,128)(2,1)} fusion(bf16[8,256,3584]{2,1,0:T(8,128)(2,1)} %param.15, bf16[8,3584,256]{2,1,0:T(8,128)(2,1)} %param.14, bf16[8,60,3584]{2,0,1:T(8,128)(2,1)S(1)} %bitcast.41, f32[8,60,256]{2,1,0:T(8,128)} %fusion.2), kind=kOutput, calls=%fused_computation.1 | convolution fusion | flops 1764065280 | bytes 36732928 | tf_op jit(solution)/shard_map/erf,efd->erd/dot_general | solution.py:62
  156.3 5.7 %copy.35 = bf16[8,60,3584]{2,0,1:T(8,128)(2,1)} copy(bf16[8,60,3584]{2,1,0:T(8,128)(2,1)} %convolution_convert_fusion) | data formatting | bytes 6881280 | tf_op jit(solution)/shard_map/convert_element_type | solution.py:64
  162.0 3.9 %all-to-all-start.1 = ((bf16[8,60,3584]{2,0,1:T(8,128)(2,1)}), bf16[8,60,3584]{2,0,1:T(8,128)(2,1)S(1)}, u32[]{:S(2)}, u32[]{:S(2)}) async-start(bf16[8,60,3584]{2,0,1:T(8,128)(2,1)} %copy.35), calls=%async_computation.1 | async-start | bytes 6881280 | tf_op jit(solution)/shard_map/all_to_all | solution.py:65
  165.8 0.3 reduce-scatter.4.cloned.1.call-start
  166.1 0.1 reshape.39
  166.2 0.0 copy-done
  166.2 0.1 copy.37
  166.4 75.5 %all-to-all-done.1 = bf16[8,60,3584]{2,0,1:T(8,128)(2,1)S(1)} async-done(((bf16[8,60,3584]{2,0,1:T(8,128)(2,1)}), bf16[8,60,3584]{2,0,1:T(8,128)(2,1)S(1)}, u32[]{:S(2)}, u32[]{:S(2)}) %all-to-all-start.1) | async-done | bytes 3440672 | tf_op jit(solution)/shard_map/all_to_all | solution.py:65
  241.9 2.9 %copy.36 = bf16[4,8,15,3584]{3,2,1,0:T(8,128)(2,1)} copy(bf16[4,8,15,3584]{3,1,2,0:T(8,128)(2,1)S(1)} %bitcast.43) | data formatting | bytes 6881280 | tf_op jit(solution)/shard_map/all_to_all | solution.py:65
  244.8 3.3 %reshape.35 = bf16[480,3584]{1,0:T(8,128)(2,1)S(1)} reshape(bf16[4,8,15,3584]{3,2,1,0:T(8,128)(2,1)} %copy.36) | data formatting | bytes 6881280 | tf_op jit(solution)/shard_map/reshape | solution.py:66
  248.1 3.7 %gather_fusion = bf16[320,3584]{1,0:T(8,128)(2,1)} fusion(bf16[480,3584]{1,0:T(8,128)(2,1)S(1)} %reshape.35, s32[1024]{0:T(1024)S(1)} %pad_clamp_fusion), kind=kCustom, calls=%fused_computation | custom fusion | bytes 4588800 | tf_op jit(solution)/shard_map/gather | solution.py:67
  251.8 2.4 fusion.4
  254.2 1.2 copy.39
  255.4 0.0 reduce-scatter.4.cloned.1.call-update
  255.5 22.3 %reduce-scatter.4.cloned.1.call-done = bf16[896,40]{1,0:T(8,128)(2,1)} async-done(((bf16[3584,40]{1,0:T(8,128)(2,1)}), bf16[896,40]{1,0:T(8,128)(2,1)}) %reduce-scatter.4.cloned.1.call-update) | async-done | bytes 71696
  277.8 1.1 copy.40
  278.9 1.6 add_convert_fusion
  (12 shorter events, 0.2 us)
Async XLA Ops:
  6.5 29.4 %all-reduce.3.cloned.1.call-start = ((), (), s32[]{:S(2)}) async-start(), calls=%async_computation.3 | async-start | bytes 573440 | tf_op jit(solution)/shard_map/psum | solution.py:38
  162.0 4.2 %copy-start = (f32[40,8]{0,1:T(8,128)S(1)}, f32[40,8]{0,1:T(8,128)}, u32[]{:S(2)}) copy-start(f32[40,8]{0,1:T(8,128)} %param.12) | copy-start | bytes 3844
  162.0 79.9 %all-to-all-start.1 = ((bf16[8,60,3584]{2,0,1:T(8,128)(2,1)}), bf16[8,60,3584]{2,0,1:T(8,128)(2,1)S(1)}, u32[]{:S(2)}, u32[]{:S(2)}) async-start(bf16[8,60,3584]{2,0,1:T(8,128)(2,1)} %copy.35), calls=%async_computation.1 | async-start | bytes 6881280 | tf_op jit(solution)/shard_map/all_to_all | solution.py:65
  165.8 112.0 %reduce-scatter.4.cloned.1.call-start = ((), (), s32[]{:S(2)}) async-start(), calls=%async_computation.4 | async-start | bytes 1146880
Sparse Core Ops, SparseCore 0:
  9.6 26.2 all-reduce.2
  255.6 22.1 reduce-scatter.3
where the time goes:
time: 288 us; the launch traced here: 287 us
  waiting for transfers between devices  125 us (43%)
  blocking collectives  86.3 us (30%)
  matrix products  29.6 us (10%)
  local copies, waits for them, and re-layouts  24.4 us (8%)
  between operations  13.5 us (5%)
  other arithmetic  4.73 us (2%)
  starting transfers between devices  4.12 us (1%)
    all_to_all x1, blocking collectives, shards(): lax.all_to_all(send_buffer, 'expert', split_axis=0, concat_axis=1, tiled=...  86.3 us
    all_to_all x1, waiting for transfers between devices, shards(): lax.all_to_all(partial_out, 'expert', split_axis=1, concat_axis=0, tiled=...  75.5 us
    psum x1, waiting for transfers between devices, shards(): lax.psum(partial_terms.astype(jnp.bfloat16), 'tensor').astype(jnp.float32)  26.1 us
    unnamed x3, waiting for transfers between devices  23.1 us
    dot_general x1, matrix products, shards(): jnp.einsum('erf,efd->erd', expert_hidden, down_weight, preferred_element_...  16.5 us
    dot_general x1, matrix products, shards(): jnp.einsum('erd,edf->erf', received, gate_weight, preferred_element_type=...  8.42 us
  transfers between devices with their start and end apart: 3, of which 3 were waited for; matrix products, arithmetic and copies ran while one was open for 1% of the time, Pallas kernels for 0%

commit v1 on v0

--- a/solution.py
+++ b/solution.py
@@ -1,6 +1,8 @@
 import jax
 import jax.numpy as jnp
 from jax import lax
+from jax.experimental import pallas as pl
+from jax.experimental.pallas import tpu as pltpu
 from jax.sharding import PartitionSpec as P
 
 EXPERTS = 32
@@ -23,7 +25,7 @@
     return (flat_routes * CAP + slot_index).reshape(row_count, top_count)
 
 
-def shards(
+def shards_general(
     attn_terms, residual, norm_gain, routes, gate_scores, gate_weight, up_weight, down_weight
 ):
     tensor_count = lax.axis_size("tensor")
@@ -72,6 +74,319 @@
     return (own_state + combined).astype(jnp.bfloat16)
 
 
+MESH = pl.DeviceIdType.MESH
+
+
+def to_lanes(column):
+    rows = column.shape[0]
+    wide = jnp.broadcast_to(column, (rows, 128))
+    return jnp.concatenate([wide, jnp.zeros((128 - rows, 128), jnp.float32)], axis=0).T
+
+
+def layer_kernel(
+    attn_ref, residual_ref, gain_ref, routes_ref, scores_ref, gate_hbm, up_hbm, down_hbm, out_ref,
+    gate_v, up_v, down_v, attn_in, state, gathered, joined, gate_acc, up_acc, hidden_v,
+    squares, tiles, mix_v, scale_v,
+    pair_send, pair_recv, plane_send, plane_recv, back_send, back_recv,
+    weight_sem, attn_sems, square_send, square_recv, tile_send, tile_recv,
+    gather_send, gather_recv, pair_ssem, pair_rsem, plane_ssem, plane_rsem, back_ssem, back_rsem,
+):
+    depth = lax.axis_size("expert")
+    z, x, c = lax.axis_index("expert"), lax.axis_index("tensor"), lax.axis_index("pipe")
+    experts = gate_v.shape[1]
+    rows, piece = state.shape
+    sibling, across, corner = {"pipe": 1 - c}, {"tensor": 1 - x}, {"tensor": 1 - x, "pipe": 1 - c}
+    beyond = [None] + [{"expert": lax.rem(z + d, depth)} for d in range(1, depth)]
+    starts = [
+        pl.multiple_of((2 * xx + cc) * piece, 128)
+        for xx, cc in ((x, c), (x, 1 - c), (1 - x, c), (1 - x, 1 - c))
+    ]
+
+    weight_copies = {}
+    for k in range(4):
+        cut = pl.ds(starts[k], piece)
+        weight_copies["gate", k] = pltpu.make_async_copy(
+            gate_hbm.at[:, cut, :], gate_v.at[k], weight_sem.at[0, k]
+        )
+        weight_copies["up", k] = pltpu.make_async_copy(
+            up_hbm.at[:, cut, :], up_v.at[k], weight_sem.at[1, k]
+        )
+    for k in (3, 2, 1, 0):
+        weight_copies["down", k] = pltpu.make_async_copy(
+            down_hbm.at[:, :, pl.ds(starts[k], piece)], down_v.at[k], weight_sem.at[2, k]
+        )
+    for copy in weight_copies.values():
+        copy.start()
+
+    barrier = pltpu.get_barrier_semaphore()
+    partners = [sibling, across, corner] + beyond[1:]
+    for partner in partners:
+        pl.semaphore_signal(barrier, inc=1, device_id=partner, device_id_type=MESH)
+    pl.semaphore_wait(barrier, len(partners))
+
+    sends = []
+
+    def remote(source, target, send_sem, recv_sem, partner):
+        return pltpu.make_async_remote_copy(
+            src_ref=source, dst_ref=target, send_sem=send_sem, recv_sem=recv_sem,
+            device_id=partner, device_id_type=MESH,
+        )
+
+    def send(*args):
+        copy = remote(*args)
+        copy.start()
+        sends.append(copy)
+        return copy
+
+    attn_copy = send(
+        attn_ref.at[0, :, pl.ds(starts[2], piece)], attn_in, attn_sems.at[0], attn_sems.at[1], across
+    )
+    own_cut = pl.ds(starts[0], piece)
+    partial = residual_ref[:, own_cut].astype(jnp.float32) + attn_ref[0, :, own_cut].astype(jnp.float32)
+    attn_copy.wait_recv()
+    own_state = partial + attn_in[...].astype(jnp.float32)
+    state[...] = own_state
+    gathered[0, 0] = (own_state * gain_ref[:, own_cut]).astype(jnp.bfloat16)
+
+    gather_count = [0]
+
+    def gather_copy(source, slot, partner):
+        number = gather_count[0]
+        gather_count[0] += 1
+        d, k = slot
+        return send(
+            gathered.at[source], gathered.at[slot], gather_send.at[number],
+            gather_recv.at[d, k], partner,
+        )
+
+    def gather_wait(d, k):
+        remote(
+            gathered.at[d, k], gathered.at[d, k], gather_send.at[0], gather_recv.at[d, k], sibling
+        ).wait_recv()
+
+    for d in range(1, depth):
+        gather_copy((0, 0), (depth - d, 0), beyond[d])
+    gather_copy((0, 0), (0, 2), across)
+    gather_copy((0, 0), (0, 1), sibling)
+
+    squares[0] = to_lanes(jnp.sum(own_state * own_state, axis=1, keepdims=True))[:8]
+    square_copies = [
+        send(squares.at[0], squares.at[k], square_send.at[k], square_recv.at[k], partner)
+        for k, partner in ((1, sibling), (2, across), (3, corner))
+    ]
+    scores = scores_ref[...]
+    mix = ROUTE_SCALE * scores / jnp.sum(scores, axis=1, keepdims=True)
+    lanes = lax.broadcasted_iota(jnp.int32, (rows, 128), 1)
+    chosen = lax.rem(z * experts + lanes, depth * experts)
+    chosen = jnp.where(lanes < depth * experts, chosen, -1)
+    weights = jnp.zeros((rows, 128), jnp.float32)
+    for choice in range(scores.shape[1]):
+        weights = weights + jnp.where(
+            routes_ref[:, choice : choice + 1] == chosen, mix[:, choice : choice + 1], 0.0
+        )
+    turned = to_lanes(weights)
+    for copy in square_copies:
+        copy.wait_recv()
+    total = squares[0] + squares[1] + squares[2] + squares[3]
+    inverse = lax.rsqrt(total / (4 * piece) + NORM_EPS)
+    for d in range(depth):
+        tiles[d, 0, :experts] = turned[d * experts : (d + 1) * experts]
+        tiles[d, 0, experts:] = inverse
+    tile_copies = [
+        send(
+            tiles.at[d, 0], tiles.at[depth - d, 1], tile_send.at[d], tile_recv.at[depth - d],
+            beyond[d],
+        )
+        for d in range(1, depth)
+    ]
+
+    for d in range(1, depth):
+        gather_wait(d, 0)
+        gather_copy((d, 0), (d, 2), across)
+        gather_copy((d, 0), (d, 1), sibling)
+
+    for copy in tile_copies:
+        copy.wait_recv()
+    for d in range(depth):
+        tile = tiles[d, 0 if d == 0 else 1]
+        back = jnp.concatenate([tile, jnp.zeros((128 - 2 * experts, 128), jnp.float32)], axis=0).T
+        mix_v[d * rows : (d + 1) * rows] = back[:rows]
+        scale_v[d * rows : (d + 1) * rows] = jnp.broadcast_to(
+            back[:rows, experts : experts + 1], (rows, 128)
+        )
+
+    def join(k):
+        joined[k] = jnp.concatenate(
+            [gathered[d, k].astype(jnp.float32) for d in range(depth)], axis=0
+        ).astype(jnp.bfloat16)
+
+    def project(k):
+        join(k)
+        weight_copies["gate", k].wait()
+        weight_copies["up", k].wait()
+
+        def one_expert(e, carry):
+            left = joined[k]
+            gate = jnp.dot(left, gate_v[k, e], preferred_element_type=jnp.float32)
+            up = jnp.dot(left, up_v[k, e], preferred_element_type=jnp.float32)
+            if k > 0:
+                gate = gate_acc[e] + gate
+                up = up_acc[e] + up
+            if k < 3:
+                gate_acc[e] = gate
+                up_acc[e] = up
+            else:
+                lane = lax.broadcasted_iota(jnp.int32, (depth * rows, 128), 1)
+                weight = jnp.sum(jnp.where(lane == e, mix_v[...], 0.0), axis=1, keepdims=True)
+                scale = scale_v[:, :1]
+                gate = gate * scale
+                up = up * (scale * weight)
+                hidden_v[e] = (gate / (1.0 + jnp.exp(-gate)) * up).astype(jnp.bfloat16)
+            return carry
+
+        lax.fori_loop(0, experts, one_expert, 0)
+
+    project(0)
+    gather_wait(0, 2)
+    gather_copy((0, 2), (0, 3), sibling)
+    for d in range(depth):
+        gather_wait(d, 1)
+    project(1)
+    for d in range(1, depth):
+        gather_wait(d, 2)
+        gather_copy((d, 2), (d, 3), sibling)
+    project(2)
+    for d in range(depth):
+        gather_wait(d, 3)
+    project(3)
+
+    def contract(k):
+        weight_copies["down", k].wait()
+        left = jnp.concatenate([hidden_v[e] for e in range(experts)], axis=1)
+        right = down_v[k].reshape(experts * down_v.shape[2], piece)
+        return jnp.dot(left, right, preferred_element_type=jnp.float32)
+
+    def part(values, d):
+        return values[d * rows : (d + 1) * rows]
+
+    pairs = {}
+    for index, k in ((0, 3), (1, 1)):
+        values = contract(k)
+        for d in range(depth):
+            pair_send[index, d] = part(values, d).astype(jnp.bfloat16)
+        pairs[index] = send(
+            pair_send.at[index], pair_recv.at[index], pair_ssem.at[index], pair_rsem.at[index], sibling
+        )
+        if index == 0:
+            values = contract(2)
+            pairs[0].wait_recv()
+            planes = {}
+            for d in list(range(1, depth)) + [0]:
+                summed = part(values, d) + pair_recv[0, d].astype(jnp.float32)
+                plane_send[d] = summed.astype(jnp.bfloat16)
+                planes[d] = send(
+                    plane_send.at[d], plane_recv.at[d], plane_ssem.at[d], plane_rsem.at[d], across
+                )
+    values = contract(0)
+    pairs[1].wait_recv()
+    backs = []
+    for d in range(1, depth):
+        planes[d].wait_recv()
+        summed = part(values, d) + pair_recv[1, d].astype(jnp.float32)
+        summed = summed + plane_recv[d].astype(jnp.float32)
+        back_send[d] = summed.astype(jnp.bfloat16)
+        backs.append(
+            send(
+                back_send.at[d], back_recv.at[depth - d], back_ssem.at[d], back_rsem.at[depth - d],
+                beyond[d],
+            )
+        )
+    planes[0].wait_recv()
+    summed = state[...] + part(values, 0) + pair_recv[1, 0].astype(jnp.float32)
+    summed = summed + plane_recv[0].astype(jnp.float32)
+    for copy in backs:
+        copy.wait_recv()
+    for d in range(1, depth):
+        summed = summed + back_recv[d].astype(jnp.float32)
+    out_ref[...] = summed.astype(jnp.bfloat16)
+    for copy in sends:
+        copy.wait_send()
+
+
+def shards_kernel(
+    attn_terms, residual, norm_gain, routes, gate_scores, gate_weight, up_weight, down_weight
+):
+    depth = lax.axis_size("expert")
+    rows, width = residual.shape
+    piece = width // 4
+    experts, _, units = gate_weight.shape
+    bf16, f32 = jnp.bfloat16, jnp.float32
+    dma = pltpu.SemaphoreType.DMA
+    vmem, anywhere = pl.BlockSpec(memory_space=pltpu.VMEM), pl.BlockSpec(memory_space=pl.ANY)
+    flops = 6 * depth * rows * experts * width * units
+    return pl.pallas_call(
+        layer_kernel,
+        out_shape=jax.ShapeDtypeStruct((rows, piece), bf16),
+        in_specs=[vmem] * 5 + [anywhere] * 3,
+        out_specs=vmem,
+        scratch_shapes=[
+            pltpu.VMEM((4, experts, piece, units), bf16),
+            pltpu.VMEM((4, experts, piece, units), bf16),
+            pltpu.VMEM((4, experts, units, piece), bf16),
+            pltpu.VMEM((rows, piece), bf16),
+            pltpu.VMEM((rows, piece), f32),
+            pltpu.VMEM((depth, 4, rows, piece), bf16),
+            pltpu.VMEM((4, depth * rows, piece), bf16),
+            pltpu.VMEM((experts, depth * rows, units), f32),
+            pltpu.VMEM((experts, depth * rows, units), f32),
+            pltpu.VMEM((experts, depth * rows, units), bf16),
+            pltpu.VMEM((4, 8, 128), f32),
+            pltpu.VMEM((depth, 2, 2 * experts, 128), f32),
+            pltpu.VMEM((depth * rows, 128), f32),
+            pltpu.VMEM((depth * rows, 128), f32),
+            pltpu.VMEM((2, depth, rows, piece), bf16),
+            pltpu.VMEM((2, depth, rows, piece), bf16),
+            pltpu.VMEM((depth, rows, piece), bf16),
+            pltpu.VMEM((depth, rows, piece), bf16),
+            pltpu.VMEM((depth, rows, piece), bf16),
+            pltpu.VMEM((depth, rows, piece), bf16),
+            dma((3, 4)),
+            dma((2,)),
+            dma((4,)),
+            dma((4,)),
+            dma((depth,)),
+            dma((depth,)),
+            dma((4 * depth,)),
+            dma((depth, 4)),
+            dma((2,)),
+            dma((2,)),
+            dma((depth,)),
+            dma((depth,)),
+            dma((depth,)),
+            dma((depth,)),
+        ],
+        compiler_params=pltpu.CompilerParams(
+            collective_id=0, has_side_effects=True, vmem_limit_bytes=62 * 1024 * 1024
+        ),
+        cost_estimate=pl.CostEstimate(
+            flops=flops, bytes_accessed=6 * experts * width * units, transcendentals=0
+        ),
+        name="routed_layer",
+    )(
+        attn_terms, residual, norm_gain[None, :], routes, gate_scores,
+        gate_weight, up_weight, down_weight,
+    )
+
+
+def shards(attn_terms, residual, *rest):
+    four_owners = lax.axis_size("tensor") == 2 and lax.axis_size("pipe") == 2
+    small = lax.axis_size("expert") <= 4 and rest[3].shape[0] == 8
+    whole_tiles = residual.shape[0] % 8 == 0 and residual.shape[1] % 512 == 0
+    if four_owners and small and whole_tiles:
+        return shards_kernel(attn_terms, residual, *rest)
+    return shards_general(attn_terms, residual, *rest)
+
+
 def solution(mesh):
     placed = (
         P("tensor", ("group", "expert"), None),

time: 288 us -> 50.2 us (0.17)
  waiting for transfers between devices: 125 us -> 0 us
  blocking collectives: 86.3 us -> 0 us
  Pallas kernels: 0 us -> 44.3 us
  matrix products: 29.6 us -> 0 us
  local copies, waits for them, and re-layouts: 24.4 us -> 5.59 us
  between operations: 13.5 us -> 0.01 us
  other arithmetic: 4.73 us -> 0 us
  starting transfers between devices: 4.12 us -> 0 us
    all_to_all x1 -> x0, blocking collectives: 86.3 us -> none  [shards(): lax.all_to_all(send_buffer, 'expert', split_axis=0, concat_axis=1, tiled=...]
    all_to_all x1 -> x0, waiting for transfers between devices: 75.5 us -> none  [shards(): lax.all_to_all(partial_out, 'expert', split_axis=1, concat_axis=0, tiled=...]
    pallas_call x0 -> x1, Pallas kernels: none -> 44.3 us  [shards_kernel(): pl.pallas_call(layer_kernel, out_shape=jax.ShapeDtypeStruct((rows, piece)...]
    dot_general x4 -> x0, matrix products: 29.6 us -> none  [the longest x1 16.5 us: shards(): jnp.einsum('erf,efd->erd', expert_hidden, down_weight, preferred_element_...]
    psum x1 -> x0, waiting for transfers between devices: 26.1 us -> none  [shards(): lax.psum(partial_terms.astype(jnp.bfloat16), 'tensor').astype(jnp.float32)]
    unnamed x3 -> x0, waiting for transfers between devices: 23.1 us -> none
    reshape x2 -> x0, local copies, waits for them, and re-layouts: 6.04 us -> none  [the longest x1 3.28 us: shards(): flat_rows = returned.reshape(EXPERTS * CAP, returned.shape[2])]
    convert_element_type x1 -> x0, local copies, waits for them, and re-layouts: 5.7 us -> none  [shards(): partial_out = jnp.einsum('erf,efd->erd', expert_hidden, down_weight, pref...]
  transfers between devices with their start and end apart: 3 -> 0, of which waited for: 3 -> 0; matrix products, arithmetic and copies ran while one was open for 1% -> 0% of each run, Pallas kernels for 0% -> 0%
where the time goes in v1:
time: 50.2 us; the launch traced here: 49.9 us
  Pallas kernels  44.3 us (88%)
  local copies, waits for them, and re-layouts  5.59 us (11%)
    pallas_call x1, Pallas kernels, shards_kernel(): pl.pallas_call(layer_kernel, out_shape=jax.ShapeDtypeStruct((rows, piece)...  44.3 us
    unnamed x3, local copies, waits for them, and re-layouts  4.26 us
    broadcast_in_dim x1, local copies, waits for them, and re-layouts, shards_kernel(): norm_gain[None, :]  1.33 us

profile of v1, /device:TPU:0, one launch (start us, length us, event | category | flops | bytes accessed | tf_op | source)
XLA Modules:
  0.0 49.9 jit_solution(5928004917154978515)
XLA Ops:
  0.0 1.3 %broadcast_in_dim.3.gain_ref = f32[1,3584]{1,0:T(1,128)} reshape(f32[3584]{0:T(1024)} %param.10) | data formatting | bytes 28672 | tf_op jit(solution)/shard_map/broadcast_in_dim | solution.py:376
  1.3 1.4 %copy.9.routes_ref = s32[40,8]{1,0:T(8,128)} copy(s32[40,8]{0,1:T(8,128)} %param.11) | data formatting | bytes 2560 | tf_op args[3]
  2.7 1.4 %copy.10.scores_ref = f32[40,8]{1,0:T(8,128)} copy(f32[40,8]{0,1:T(8,128)} %param.12) | data formatting | bytes 2560 | tf_op args[4]
  4.1 44.3 %routed_layer.1 = bf16[40,896]{1,0:T(8,128)(2,1)} custom-call(bf16[1,40,3584]{2,1,0:T(8,128)(2,1)} %attn_ref.1, bf16[40,3584]{1,0:T(8,128)(2,1)} %residual_ref.1, f32[1,3584]{1,0:T(1,128)} %broadcast_in_dim.3.gain_ref, s32[40,8]{1,0:T(8,128)} %copy.9.routes_ref, f32[40,8]{1,0:T(8,128)} %copy.10.scores_ref, bf16[8,3584,256]{2,1,0:T(8,128)(2,1)} %gate_hbm.1, ...), custom_call_target="tpu_custom_call" | custom-call | flops 7046430720 | bytes 44040192 | tf_op jit(solution)/shard_map/routed_layer/pallas_call | solution.py:327
  48.4 1.5 %copy.12 = bf16[40,896]{1,0:T(8,128)(2,1)} copy(bf16[40,896]{1,0:T(8,128)(2,1)} %routed_layer.1) | data formatting | bytes 143360

commit v2 on v1

--- a/solution.py
+++ b/solution.py
@@ -85,10 +85,10 @@
 
 def layer_kernel(
     attn_ref, residual_ref, gain_ref, routes_ref, scores_ref, gate_hbm, up_hbm, down_hbm, out_ref,
-    gate_v, up_v, down_v, attn_in, state, gathered, joined, gate_acc, up_acc, hidden_v,
-    squares, tiles, mix_v, scale_v,
+    gate_v, up_v, down_v, attn_in, own_in, state, gathered, joined, gate_acc, up_acc, hidden_v,
+    squares, tiles, tiles_in, mix_v, scale_v,
     pair_send, pair_recv, plane_send, plane_recv, back_send, back_recv,
-    weight_sem, attn_sems, square_send, square_recv, tile_send, tile_recv,
+    weight_sem, own_sem, attn_sems, square_send, square_recv, tile_send, tile_recv,
     gather_send, gather_recv, pair_ssem, pair_rsem, plane_ssem, plane_rsem, back_ssem, back_rsem,
 ):
     depth = lax.axis_size("expert")
@@ -102,28 +102,37 @@
         for xx, cc in ((x, c), (x, 1 - c), (1 - x, c), (1 - x, 1 - c))
     ]
 
+    own_copies = [
+        pltpu.make_async_copy(source.at[:, pl.ds(start, piece)], own_in.at[i], own_sem.at[i])
+        for i, (source, start) in enumerate(
+            ((attn_ref.at[0], starts[2]), (attn_ref.at[0], starts[0]), (residual_ref, starts[0]))
+        )
+    ]
+    for copy in own_copies:
+        copy.start()
     weight_copies = {}
     for k in range(4):
         cut = pl.ds(starts[k], piece)
         weight_copies["gate", k] = pltpu.make_async_copy(
-            gate_hbm.at[:, cut, :], gate_v.at[k], weight_sem.at[0, k]
+            gate_hbm.at[:, cut, :], gate_v.at[k // 2, :, pl.ds(k % 2 * piece, piece)], weight_sem.at[0, k]
         )
         weight_copies["up", k] = pltpu.make_async_copy(
-            up_hbm.at[:, cut, :], up_v.at[k], weight_sem.at[1, k]
+            up_hbm.at[:, cut, :], up_v.at[k // 2, :, pl.ds(k % 2 * piece, piece)], weight_sem.at[1, k]
         )
     for k in (3, 2, 1, 0):
         weight_copies["down", k] = pltpu.make_async_copy(
             down_hbm.at[:, :, pl.ds(starts[k], piece)], down_v.at[k], weight_sem.at[2, k]
         )
-    for copy in weight_copies.values():
-        copy.start()
-
     barrier = pltpu.get_barrier_semaphore()
     partners = [sibling, across, corner] + beyond[1:]
     for partner in partners:
         pl.semaphore_signal(barrier, inc=1, device_id=partner, device_id_type=MESH)
+    for copy in weight_copies.values():
+        copy.start()
     pl.semaphore_wait(barrier, len(partners))
 
+    order = sorted(range(1, depth), key=lambda d: (min(d, depth - d), d))
+    arrivals = [depth - d for d in order]
     sends = []
 
     def remote(source, target, send_sem, recv_sem, partner):
@@ -138,15 +147,21 @@
         sends.append(copy)
         return copy
 
+    own_copies[0].wait()
     attn_copy = send(
-        attn_ref.at[0, :, pl.ds(starts[2], piece)], attn_in, attn_sems.at[0], attn_sems.at[1], across
-    )
-    own_cut = pl.ds(starts[0], piece)
-    partial = residual_ref[:, own_cut].astype(jnp.float32) + attn_ref[0, :, own_cut].astype(jnp.float32)
+        own_in.at[0], attn_in, attn_sems.at[0], attn_sems.at[1], across
+    )
+    own_copies[1].wait()
+    own_copies[2].wait()
+    gain_rows = piece // 128
+    gain = jnp.concatenate(
+        [gain_ref[pl.ds((2 * x + c) * gain_rows + i, 1), :] for i in range(gain_rows)], axis=1
+    )
+    partial = own_in[1].astype(jnp.float32) + own_in[2].astype(jnp.float32)
     attn_copy.wait_recv()
     own_state = partial + attn_in[...].astype(jnp.float32)
     state[...] = own_state
-    gathered[0, 0] = (own_state * gain_ref[:, own_cut]).astype(jnp.bfloat16)
+    gathered[0, 0] = (own_state * gain).astype(jnp.bfloat16)
 
     gather_count = [0]
 
@@ -164,9 +179,9 @@
             gathered.at[d, k], gathered.at[d, k], gather_send.at[0], gather_recv.at[d, k], sibling
         ).wait_recv()
 
-    for d in range(1, depth):
+    gather_copy((0, 0), (0, 2), across)
+    for d in order:
         gather_copy((0, 0), (depth - d, 0), beyond[d])
-    gather_copy((0, 0), (0, 2), across)
     gather_copy((0, 0), (0, 1), sibling)
 
     squares[0] = to_lanes(jnp.sum(own_state * own_state, axis=1, keepdims=True))[:8]
@@ -175,90 +190,93 @@
         for k, partner in ((1, sibling), (2, across), (3, corner))
     ]
     scores = scores_ref[...]
-    mix = ROUTE_SCALE * scores / jnp.sum(scores, axis=1, keepdims=True)
-    lanes = lax.broadcasted_iota(jnp.int32, (rows, 128), 1)
-    chosen = lax.rem(z * experts + lanes, depth * experts)
-    chosen = jnp.where(lanes < depth * experts, chosen, -1)
-    weights = jnp.zeros((rows, 128), jnp.float32)
-    for choice in range(scores.shape[1]):
-        weights = weights + jnp.where(
-            routes_ref[:, choice : choice + 1] == chosen, mix[:, choice : choice + 1], 0.0
-        )
-    turned = to_lanes(weights)
+    mix = ROUTE_SCALE * scores / jnp.sum(scores, axis=0, keepdims=True)
+    first = lax.broadcasted_iota(jnp.int32, (experts, rows), 0)
+    tiles[...] = jnp.zeros_like(tiles)
+    for d in range(depth):
+        chosen = lax.rem(z + d, depth) * experts + first
+        weights = jnp.zeros((experts, rows), jnp.float32)
+        for choice in range(scores.shape[0]):
+            weights = weights + jnp.where(
+                routes_ref[choice : choice + 1, :] == chosen, mix[choice : choice + 1, :], 0.0
+            )
+        tiles[d, :experts, :rows] = weights
     for copy in square_copies:
         copy.wait_recv()
     total = squares[0] + squares[1] + squares[2] + squares[3]
     inverse = lax.rsqrt(total / (4 * piece) + NORM_EPS)
     for d in range(depth):
-        tiles[d, 0, :experts] = turned[d * experts : (d + 1) * experts]
-        tiles[d, 0, experts:] = inverse
+        tiles[d, experts:, :] = inverse
     tile_copies = [
         send(
-            tiles.at[d, 0], tiles.at[depth - d, 1], tile_send.at[d], tile_recv.at[depth - d],
+            tiles.at[d], tiles_in.at[depth - d], tile_send.at[d], tile_recv.at[depth - d],
             beyond[d],
         )
         for d in range(1, depth)
     ]
 
-    for d in range(1, depth):
+    for d in arrivals:
         gather_wait(d, 0)
         gather_copy((d, 0), (d, 2), across)
         gather_copy((d, 0), (d, 1), sibling)
 
+    def join(half):
+        for i in range(2):
+            joined[half, :, i * piece : (i + 1) * piece] = jnp.concatenate(
+                [gathered[d, 2 * half + i].astype(jnp.float32) for d in range(depth)], axis=0
+            ).astype(jnp.bfloat16)
+
+    def project_first(e, carry):
+        left = joined[0]
+        gate_acc[e] = jnp.dot(left, gate_v[0, e], preferred_element_type=jnp.float32)
+        up_acc[e] = jnp.dot(left, up_v[0, e], preferred_element_type=jnp.float32)
+        return carry
+
+    def project_last(e, carry):
+        left = joined[1]
+        lane = lax.broadcasted_iota(jnp.int32, (depth * rows, 128), 1)
+        weight = jnp.sum(jnp.where(lane == e, mix_v[...], 0.0), axis=1, keepdims=True)
+        scale = scale_v[:, :1]
+        gate = gate_acc[e] + jnp.dot(left, gate_v[1, e], preferred_element_type=jnp.float32)
+        up = up_acc[e] + jnp.dot(left, up_v[1, e], preferred_element_type=jnp.float32)
+        gate = gate * scale
+        up = up * (scale * weight)
+        hidden_v[e] = (gate / (1.0 + jnp.exp(-gate)) * up).astype(jnp.bfloat16)
+        return carry
+
+    def weights_wait(half):
+        for k in (2 * half, 2 * half + 1):
+            weight_copies["gate", k].wait()
+            weight_copies["up", k].wait()
+
+    def forward(d):
+        gather_wait(d, 2)
+        gather_copy((d, 2), (d, 3), sibling)
+
+    for d in [0] + arrivals:
+        gather_wait(d, 1)
+    join(0)
+    weights_wait(0)
+    lax.fori_loop(0, experts // 2, project_first, 0)
+    forward(0)
+    forward(arrivals[0])
     for copy in tile_copies:
         copy.wait_recv()
     for d in range(depth):
-        tile = tiles[d, 0 if d == 0 else 1]
+        tile = tiles[d] if d == 0 else tiles_in[d]
         back = jnp.concatenate([tile, jnp.zeros((128 - 2 * experts, 128), jnp.float32)], axis=0).T
         mix_v[d * rows : (d + 1) * rows] = back[:rows]
         scale_v[d * rows : (d + 1) * rows] = jnp.broadcast_to(
             back[:rows, experts : experts + 1], (rows, 128)
         )
-
-    def join(k):
-        joined[k] = jnp.concatenate(
-            [gathered[d, k].astype(jnp.float32) for d in range(depth)], axis=0
-        ).astype(jnp.bfloat16)
-
-    def project(k):
-        join(k)
-        weight_copies["gate", k].wait()
-        weight_copies["up", k].wait()
-
-        def one_expert(e, carry):
-            left = joined[k]
-            gate = jnp.dot(left, gate_v[k, e], preferred_element_type=jnp.float32)
-            up = jnp.dot(left, up_v[k, e], preferred_element_type=jnp.float32)
-            if k > 0:
-                gate = gate_acc[e] + gate
-                up = up_acc[e] + up
-            if k < 3:
-                gate_acc[e] = gate
-                up_acc[e] = up
-            else:
-                lane = lax.broadcasted_iota(jnp.int32, (depth * rows, 128), 1)
-                weight = jnp.sum(jnp.where(lane == e, mix_v[...], 0.0), axis=1, keepdims=True)
-                scale = scale_v[:, :1]
-                gate = gate * scale
-                up = up * (scale * weight)
-                hidden_v[e] = (gate / (1.0 + jnp.exp(-gate)) * up).astype(jnp.bfloat16)
-            return carry
-
-        lax.fori_loop(0, experts, one_expert, 0)
-
-    project(0)
-    gather_wait(0, 2)
-    gather_copy((0, 2), (0, 3), sibling)
-    for d in range(depth):
-        gather_wait(d, 1)
-    project(1)
-    for d in range(1, depth):
-        gather_wait(d, 2)
-        gather_copy((d, 2), (d, 3), sibling)
-    project(2)
+    lax.fori_loop(experts // 2, experts, project_first, 0)
+    for d in arrivals[1:]:
+        forward(d)
     for d in range(depth):
         gather_wait(d, 3)
-    project(3)
+    join(1)
+    weights_wait(1)
+    lax.fori_loop(0, experts, project_last, 0)
 
     def contract(k):
         weight_copies["down", k].wait()
@@ -327,21 +345,23 @@
     return pl.pallas_call(
         layer_kernel,
         out_shape=jax.ShapeDtypeStruct((rows, piece), bf16),
-        in_specs=[vmem] * 5 + [anywhere] * 3,
+        in_specs=[anywhere] * 2 + [vmem] * 3 + [anywhere] * 3,
         out_specs=vmem,
         scratch_shapes=[
-            pltpu.VMEM((4, experts, piece, units), bf16),
-            pltpu.VMEM((4, experts, piece, units), bf16),
+            pltpu.VMEM((2, experts, 2 * piece, units), bf16),
+            pltpu.VMEM((2, experts, 2 * piece, units), bf16),
             pltpu.VMEM((4, experts, units, piece), bf16),
             pltpu.VMEM((rows, piece), bf16),
+            pltpu.VMEM((3, rows, piece), bf16),
             pltpu.VMEM((rows, piece), f32),
             pltpu.VMEM((depth, 4, rows, piece), bf16),
-            pltpu.VMEM((4, depth * rows, piece), bf16),
+            pltpu.VMEM((2, depth * rows, 2 * piece), bf16),
             pltpu.VMEM((experts, depth * rows, units), f32),
             pltpu.VMEM((experts, depth * rows, units), f32),
             pltpu.VMEM((experts, depth * rows, units), bf16),
             pltpu.VMEM((4, 8, 128), f32),
-            pltpu.VMEM((depth, 2, 2 * experts, 128), f32),
+            pltpu.VMEM((depth, 2 * experts, 128), f32),
+            pltpu.VMEM((depth, 2 * experts, 128), f32),
             pltpu.VMEM((depth * rows, 128), f32),
             pltpu.VMEM((depth * rows, 128), f32),
             pltpu.VMEM((2, depth, rows, piece), bf16),
@@ -351,6 +371,7 @@
             pltpu.VMEM((depth, rows, piece), bf16),
             pltpu.VMEM((depth, rows, piece), bf16),
             dma((3, 4)),
+            dma((3,)),
             dma((2,)),
             dma((4,)),
             dma((4,)),
@@ -373,7 +394,7 @@
         ),
         name="routed_layer",
     )(
-        attn_terms, residual, norm_gain[None, :], routes, gate_scores,
+        attn_terms, residual, norm_gain.reshape(width // 128, 128), routes.T, gate_scores.T,
         gate_weight, up_weight, down_weight,
     )
 

time: 50.2 us -> 43.6 us (0.87)
  local copies, waits for them, and re-layouts: 5.59 us -> 1.52 us
  Pallas kernels: 44.3 us -> 41.8 us
    unnamed x3 -> x1, local copies, waits for them, and re-layouts: 4.26 us -> 1.52 us
    pallas_call x1, Pallas kernels: 44.3 us -> 41.8 us  [shards_kernel(): pl.pallas_call(layer_kernel, out_shape=jax.ShapeDtypeStruct((rows, piece)...]
    broadcast_in_dim x1 -> x0, local copies, waits for them, and re-layouts: 1.33 us -> none  [shards_kernel(): norm_gain[None, :]]
where the time goes in v2:
time: 43.6 us; the launch traced here: 43.4 us
  Pallas kernels  41.8 us (96%)
  local copies, waits for them, and re-layouts  1.52 us (3%)
    pallas_call x1, Pallas kernels, shards_kernel(): pl.pallas_call(layer_kernel, out_shape=jax.ShapeDtypeStruct((rows, piece)...  41.8 us
    unnamed x1, local copies, waits for them, and re-layouts  1.52 us

profile of v2, /device:TPU:0, one launch (start us, length us, event | category | flops | bytes accessed | tf_op | source)
XLA Modules:
  0.0 43.4 jit_solution(5615439359871128915)
XLA Ops:
  0.0 41.8 %routed_layer.1 = bf16[40,896]{1,0:T(8,128)(2,1)} custom-call(bf16[1,40,3584]{2,1,0:T(8,128)(2,1)} %attn_ref.1, bf16[40,3584]{1,0:T(8,128)(2,1)} %residual_ref.1, f32[28,128]{1,0:T(8,128)} %bitcast.3, s32[8,40]{1,0:T(8,128)} %bitcast.4, f32[8,40]{1,0:T(8,128)} %bitcast.5, bf16[8,3584,256]{2,1,0:T(8,128)(2,1)} %gate_hbm.1, bf16[8,3584,256]{2,1,0:T(8,128)(2,1)} %up_hbm.1, ...), custom_call_target="tpu_custom_call" | custom-call | flops 7046430720 | bytes 44040192 | tf_op jit(solution)/shard_map/routed_layer/pallas_call | solution.py:345
  41.9 1.5 %copy.10 = bf16[40,896]{1,0:T(8,128)(2,1)} copy(bf16[40,896]{1,0:T(8,128)(2,1)} %routed_layer.1) | data formatting | bytes 143360

commit v3 on v2

--- a/solution.py
+++ b/solution.py
@@ -234,8 +234,7 @@
 
     def project_last(e, carry):
         left = joined[1]
-        lane = lax.broadcasted_iota(jnp.int32, (depth * rows, 128), 1)
-        weight = jnp.sum(jnp.where(lane == e, mix_v[...], 0.0), axis=1, keepdims=True)
+        weight = mix_v[:, e : e + 1]
         scale = scale_v[:, :1]
         gate = gate_acc[e] + jnp.dot(left, gate_v[1, e], preferred_element_type=jnp.float32)
         up = up_acc[e] + jnp.dot(left, up_v[1, e], preferred_element_type=jnp.float32)
@@ -257,7 +256,7 @@
         gather_wait(d, 1)
     join(0)
     weights_wait(0)
-    lax.fori_loop(0, experts // 2, project_first, 0)
+    lax.fori_loop(0, experts // 2, project_first, 0, unroll=4)
     forward(0)
     forward(arrivals[0])
     for copy in tile_copies:
@@ -269,14 +268,15 @@
         scale_v[d * rows : (d + 1) * rows] = jnp.broadcast_to(
             back[:rows, experts : experts + 1], (rows, 128)
         )
-    lax.fori_loop(experts // 2, experts, project_first, 0)
+    lax.fori_loop(experts // 2, experts, project_first, 0, unroll=4)
     for d in arrivals[1:]:
         forward(d)
     for d in range(depth):
         gather_wait(d, 3)
     join(1)
     weights_wait(1)
-    lax.fori_loop(0, experts, project_last, 0)
+    for e in range(experts):
+        project_last(e, 0)
 
     def contract(k):
         weight_copies["down", k].wait()

time: 43.6 us -> 40 us (0.917)
  Pallas kernels: 41.8 us -> 38.3 us
    pallas_call x1, Pallas kernels: 41.8 us -> 38.3 us  [shards_kernel(): pl.pallas_call(layer_kernel, out_shape=jax.ShapeDtypeStruct((rows, piece)...]
where the time goes in v3:
time: 40 us; the launch traced here: 39.8 us
  Pallas kernels  38.3 us (96%)
  local copies, waits for them, and re-layouts  1.52 us (4%)
    pallas_call x1, Pallas kernels, shards_kernel(): pl.pallas_call(layer_kernel, out_shape=jax.ShapeDtypeStruct((rows, piece)...  38.3 us
    unnamed x1, local copies, waits for them, and re-layouts  1.52 us

profile of v3, /device:TPU:0, one launch (start us, length us, event | category | flops | bytes accessed | tf_op | source)
XLA Modules:
  0.0 39.8 jit_solution(12839222935216625652)
XLA Ops:
  0.0 38.3 %routed_layer.1 = bf16[40,896]{1,0:T(8,128)(2,1)} custom-call(bf16[1,40,3584]{2,1,0:T(8,128)(2,1)} %attn_ref.1, bf16[40,3584]{1,0:T(8,128)(2,1)} %residual_ref.1, f32[28,128]{1,0:T(8,128)} %bitcast.3, s32[8,40]{1,0:T(8,128)} %bitcast.4, f32[8,40]{1,0:T(8,128)} %bitcast.5, bf16[8,3584,256]{2,1,0:T(8,128)(2,1)} %gate_hbm.1, bf16[8,3584,256]{2,1,0:T(8,128)(2,1)} %up_hbm.1, ...), custom_call_target="tpu_custom_call" | custom-call | flops 7046430720 | bytes 44040192 | tf_op jit(solution)/shard_map/routed_layer/pallas_call | solution.py:345
  38.3 1.5 %copy.10 = bf16[40,896]{1,0:T(8,128)(2,1)} copy(bf16[40,896]{1,0:T(8,128)(2,1)} %routed_layer.1) | data formatting | bytes 143360
